TPU v7x, 32 devices: a whole 2x2x4 slice. The times are simulated.
32 devices in a mesh: groups: 2 (over y), wide: 4 (over z), narrow: 2 (over x), pol: 2 (over core).
Axes of the slice: x: 2, y: 2, z: 4, core: 2. Of those that a mesh axis runs over, the one named last changes fastest.
Arguments:
- voltages: bfloat16 [1024, 12288], P(('groups', 'narrow', 'pol'), 'wide'), parts along dimension 0, may hold values from -6 to 6
- pfb_window: float32 [4, 1024], replicated, may hold values from -0.25 to 0.25
- tile_pairs: int32 [3, 2], replicated, may hold values from 0 to 1, as said below
- assign: int32 [4, 1], replicated, may hold values from -1 to 2, as said below
Outputs:
- visibility: bfloat16 [8, 16, 256, 2, 256], P(('groups', 'wide'), ('narrow', 'pol')), parts along dimension 0
There are 2 independent parts, one for each index of `groups`. A program takes and returns all parts, laid end to end along the dimension named above; an argument that names none is the same for every part. Nothing has to cross between parts.
Inputs may be any that keep to these rules, and one draw needn't show every extreme that they name: `tile_pairs`: each row lists a distinct pair of blocks with row <= column; every such pair of the 2 blocks appears in exactly one row. `assign`: every tile number 0 .. 2 appears exactly once in the table; in each row the tile numbers come first and the remaining entries are -1; some row holds 1 tiles.
All inputs are finite; a program needn't handle non-finite values.
Results may differ from a plain program's by a relative error of at most 0.0062.
Values may be sent and summed in bfloat16 or wider, within the bound.
A program may use at most 128 MiB of HBM per device.

v0:
```python
import math

import jax
import jax.numpy as jnp
from jax import lax
from jax.sharding import PartitionSpec as P

CHAN = 512
OUTCH = 16
BLOCK = 256


def passed_along(block, axis, distance):
    devices = range(lax.axis_size(axis))
    route = [(i - distance, i) for i in devices if i - distance in devices]
    return lax.ppermute(block, axis, route)


def fourier_table(length, channels):
    sample_pos = jnp.arange(length, dtype=jnp.int32)[:, None]
    channel_pos = jnp.arange(channels, dtype=jnp.int32)[None, :]
    phase = (sample_pos * channel_pos % length).astype(jnp.float32) * (2.0 * math.pi / length)
    table = jnp.stack([jnp.cos(phase), -jnp.sin(phase)], axis=2)
    return table.reshape(length, 2 * channels).astype(jnp.bfloat16)


def tile_product(samples_in, tile_pairs, tile_number, block_width, averaged):
    safe_number = jnp.maximum(tile_number, 0)
    block_row = tile_pairs[safe_number, 0]
    block_column = tile_pairs[safe_number, 1]
    left = lax.dynamic_slice_in_dim(samples_in, block_row * block_width, block_width, 3)
    right = lax.dynamic_slice_in_dim(samples_in, block_column * block_width, block_width, 3)
    turned = jnp.stack([-right[:, 1], right[:, 0]], axis=1)
    combined = jnp.concatenate([right, turned], axis=3)
    outputs_here = left.shape[0] // averaged
    left_g = left.reshape(outputs_here, averaged, 2, left.shape[2], block_width)
    combined_g = combined.reshape(outputs_here, averaged, 2, left.shape[2], 2 * block_width)
    return jnp.einsum("ocrsi,ocrsj->oij", left_g, combined_g, preferred_element_type=jnp.float32)


def on_device(voltages, pfb_window, tile_pairs, assign):
    taps, length = pfb_window.shape
    channels = length // 2
    block_width = BLOCK
    averaged = CHAN // OUTCH
    history_rim = passed_along(voltages, "wide", 1)
    extended = jnp.concatenate([history_rim, voltages], axis=1).astype(jnp.float32)
    frames = extended.reshape(voltages.shape[0], -1, length)
    spectra_here = frames.shape[1] - taps + 1
    filtered = pfb_window[0] * frames[:, 0:spectra_here]
    for tap_index in range(1, taps):
        filtered = (
            filtered + pfb_window[tap_index] * frames[:, tap_index : tap_index + spectra_here]
        )
    filtered = filtered.astype(jnp.bfloat16)
    table = fourier_table(length, channels)
    spectra = jnp.einsum("imk,kq->qmi", filtered, table, preferred_element_type=jnp.float32).astype(
        jnp.bfloat16
    )
    moved = lax.all_to_all(
        spectra[:, :, None, :], ("narrow", "pol"), split_axis=0, concat_axis=2, tiled=True
    )
    arranged = moved.reshape(moved.shape[0] // 2, 2, spectra_here, -1)
    outputs_here = arranged.shape[0] // averaged
    position = lax.axis_index("wide")
    wide_count = lax.axis_size("wide")
    slots = assign.shape[1]
    own_row = lax.dynamic_index_in_dim(assign, position, 0, keepdims=False)
    scale = 1.0 / (wide_count * spectra_here * averaged)
    blank = jnp.zeros((outputs_here, block_width, 2 * block_width), jnp.float32)
    whole = lax.all_gather(arranged, "wide", axis=2, tiled=True)
    results = []
    for slot_index in range(slots):
        results.append(
            lax.cond(
                own_row[slot_index] >= 0,
                lambda number: tile_product(whole, tile_pairs, number, block_width, averaged),
                lambda number: blank,
                own_row[slot_index],
            )
        )
    totals = jnp.stack(results)
    visible = (
        (totals * scale)
        .reshape(slots, outputs_here, block_width, 2, block_width)
        .astype(jnp.bfloat16)
    )
    return visible


def solution(mesh):
    in_specs = (P(("groups", "narrow", "pol"), "wide"), P(), P(), P())
    out_specs = P(("groups", "wide"), ("narrow", "pol"), None, None, None)
    return jax.shard_map(
        on_device, mesh=mesh, in_specs=in_specs, out_specs=out_specs, check_vma=False
    )
```

profile of v0, /device:TPU:0, one launch (start us, length us, event | category | flops | bytes accessed | tf_op | source)
XLA Modules:
  0.0 131.7 jit_solution(17700605763519981718)
XLA Ops:
  6.5 0.0 copy-start
  6.5 0.0 all-gather.2.cloned.1.call-start
  6.5 1.5 %copy.31 = bf16[128,3072]{0,1:T(8,128)(2,1)S(1)} copy(bf16[128,3072]{1,0:T(8,128)(2,1)} %param.6) | data formatting | bytes 1572864 | tf_op args[0]
  8.1 5.8 %collective-permute-start = (bf16[128,3072]{0,1:T(8,128)(2,1)S(1)}, bf16[128,3072]{0,1:T(8,128)(2,1)}, u32[]{:S(2)}, u32[]{:S(2)}) collective-permute-start(bf16[128,3072]{0,1:T(8,128)(2,1)S(1)} %copy.31), channel_id=1, source_target_pairs={{0,4},{4,8},{8,12},{1,5},{5,9},{9,13},{2,6},{6,10},{10,14},{3,7},{... | collective-permute-start | bytes 2359304 | tf_op jit(solution)/shard_map/ppermute | solution.py:16
  13.9 8.5 %negate_convert_fusion = (bf16[1024,512,1]{1,0,2:T(8,128)(2,1)S(1)}, bf16[1024,512,1]{1,0,2:T(8,128)(2,1)S(1)}) fusion(), kind=kLoop, calls=%fused_computation.16 | loop fusion | flops 8912896 | bytes 2097152 | tf_op jit(solution)/shard_map/convert.1
  22.4 0.2 pad_maximum_fusion
  22.6 4.0 %copy.30 = bf16[1024,512,2]{0,2,1:T(2,128)(2,1)} copy(bf16[1024,512,2]{1,0,2:T(8,128)(2,1)S(1)} %pad_maximum_fusion) | data formatting | bytes 4194304 | tf_op jit(solution)/shard_map/stack | solution.py:23
  26.7 0.0 copy-start.2
  26.7 2.8 %reshape.113 = bf16[1024,1024,1]{0,1,2:T(8,128)(2,1)S(1)} reshape(bf16[1024,512,2]{0,2,1:T(2,128)(2,1)} %copy.30) | data formatting | bytes 4194304 | tf_op jit(solution)/shard_map/convert_element_type | solution.py:24
  29.5 0.0 copy-done.2
  29.5 0.3 collective-permute-done
  29.8 1.3 %maximum_convert_fusion = f32[128,6,1024]{0,2,1:T(8,128)S(1)} fusion(bf16[128,3,1024]{0,2,1:T(8,128)(2,1)S(1)} %bitcast.31, bf16[128,3,1024]{0,2,1:T(8,128)(2,1)} %bitcast.8), kind=kLoop, calls=%fused_computation.29 | loop fusion | flops 1572864 | bytes 4718592 | tf_op jit(solution)/shard_map/convert_element_type | solution.py:47
  31.1 1.5 %fusion.10 = bf16[1024,3,1,128]{3,0,1,2:T(8,128)(2,1)S(1)} fusion(bf16[1024,1024,1]{0,1,2:T(8,128)(2,1)S(1)} %reshape.113, f32[128,6,1024]{0,2,1:T(8,128)S(1)} %maximum_convert_fusion, f32[1024]{0:T(1024)S(1)} %bitcast.37, f32[1024]{0:T(1024)S(1)} %bitcast.38, f32[1024]{0:T(1024)S(1)} %bitcast.36, f32[1024]{0:T(1024)S(1)} %bitcast.35), kind=kOutput, calls=%fused_computation.31 | convolution fusion | flops 808845312 | bytes 9191424 | tf_op jit(solution)/shard_map/imk,kq->qmi/dot_general | solution.py:57
  32.6 0.7 copy.34
  33.3 17.0 %all_to_all.15 = bf16[1024,3,1,128]{3,1,2,0:T(4,128)(2,1)S(1)} all-to-all(bf16[1024,3,1,128]{3,1,2,0:T(4,128)(2,1)S(1)} %copy.34), channel_id=1, replica_groups=mesh['groups'=2,'wide'=4,'narrow'=2,'pol'=2] {'narrow','pol'}, dimensions={0} | all-to-all | bytes 1572864 | tf_op jit(solution)/shard_map/all_to_all | solution.py:60
  50.3 0.7 copy.45
  51.0 0.0 copy-start.3
  51.1 0.3 reshape.111
  51.4 1.0 copy.36
  52.3 0.0 all-gather.2.cloned.1.call-update
  52.4 0.0 copy-done
  52.4 0.6 constant_dynamic-slice_fusion.5
  53.6 63.7 %all-gather.2.cloned.1.call-done = bf16[128,2,12,512]{3,0,1,2:T(8,128)(2,1)} async-done(((bf16[128,2,3,512]{3,0,1,2:T(8,128)(2,1)}), bf16[128,2,12,512]{3,0,1,2:T(8,128)(2,1)}) %all-gather.2.cloned.1.call-update) | async-done | bytes 3145744 | tf_op jit(solution)/shard_map/all_gather | solution.py:71
  117.3 0.0 copy-done.3
  117.3 6.0 %conditional.1 = (f32[4,256,512]{2,1,0:T(8,128)S(1)}) conditional(s32[]{:T(128)} %convert_element_type.50, () %tuple.11, (s32[]{:T(128)}, s32[3,2]{0,1:T(2,128)S(1)}, bf16[128,2,12,512]{3,0,1,2:T(8,128)(2,1)}) %tuple.28), branch_computations={%region_0.1_spmd, %region_1.2_spmd} | conditional | flops 815923200 | bytes 35127484 | solution.py:75
  117.3 0.0 copy-start.1
  118.1 0.7 constant_dynamic-slice_fusion.4
  120.1 1.6 %dynamic-slice_negate_fusion = (bf16[128,1,12,256]{3,0,2,1:T(8,128)(2,1)S(1)}, bf16[128,1,12,256]{3,0,2,1:T(8,128)(2,1)S(1)}) fusion(s32[]{:T(128)S(6)} %add.45, s32[]{:T(128)S(6)} %select_n.28, bf16[128,2,12,512]{3,0,1,2:T(8,128)(2,1)} %get-tuple-element.30), kind=kLoop, calls=%fused_computation.2 | loop fusion | flops 1179648 | bytes 3145736 | tf_op jit(solution)/shard_map/cond/branch_1_fun/neg | solution.py:33
  121.8 0.0 copy-done.1
  121.8 0.3 constant_dynamic-slice_fusion.1
  122.1 0.3 maximum_maximum_fusion
  122.4 1.0 convolution_bitcast_fusion
  123.4 0.3 multiply_convert_fusion
  123.7 1.1 convert_element_type.58
  (1 shorter events, 0.0 us)
Async XLA Ops:
  6.5 45.8 %copy-start = (s32[4,1]{0,1:T(1,128)S(1)}, s32[4,1]{0,1:T(1,128)}, u32[]{:S(2)}) copy-start(s32[4,1]{0,1:T(1,128)} %param.9) | copy-start | bytes 52
  6.5 110.8 %all-gather.2.cloned.1.call-start = ((), (), s32[]{:S(2)}) async-start(), calls=%async_computation.1 | async-start | bytes 3932160 | tf_op jit(solution)/shard_map/all_gather | solution.py:71
  8.1 21.7 %collective-permute-start = (bf16[128,3072]{0,1:T(8,128)(2,1)S(1)}, bf16[128,3072]{0,1:T(8,128)(2,1)}, u32[]{:S(2)}, u32[]{:S(2)}) collective-permute-start(bf16[128,3072]{0,1:T(8,128)(2,1)S(1)} %copy.31), channel_id=1, source_target_pairs={{0,4},{4,8},{8,12},{1,5},{5,9},{9,13},{2,6},{6,10},{10,14},{3,7},{... | collective-permute-start | bytes 2359304 | tf_op jit(solution)/shard_map/ppermute | solution.py:16
  26.7 2.8 %copy-start.2 = (f32[4,1024]{1,0:T(4,128)S(1)}, f32[4,1024]{1,0:T(4,128)}, u32[]{:S(2)}) copy-start(f32[4,1024]{1,0:T(4,128)} %param.7) | copy-start | bytes 49156
  51.0 66.3 %copy-start.3 = (s32[3,2]{0,1:T(2,128)S(1)}, s32[3,2]{0,1:T(2,128)}, u32[]{:S(2)}) copy-start(s32[3,2]{0,1:T(2,128)} %param.8) | copy-start | bytes 76
  117.3 4.4 %copy-start.1 = (bf16[128,2,12,512]{3,0,1,2:T(8,128)(2,1)S(1)}, bf16[128,2,12,512]{3,0,1,2:T(8,128)(2,1)}, u32[]{:S(2)}) copy-start(bf16[128,2,12,512]{3,0,1,2:T(8,128)(2,1)} %get-tuple-element.30) | copy-start | bytes 9437188 | tf_op jit(solution)/shard_map/cond
Sparse Core Ops, SparseCore 0:
  52.5 64.8 all-gather.1
where the time goes:
time: 132 us
  waiting for transfers between devices  64 us (48%)
  blocking collectives  17 us (13%)
  between operations  14.1 us (11%)
  local copies, waits for them, and re-layouts  13.7 us (10%)
  other arithmetic  12.3 us (9%)
  starting transfers between devices  5.84 us (4%)
  matrix products  2.48 us (2%)
  loops' own time  2.16 us (2%)
    all_gather x1, waiting for transfers between devices, on_device(): whole = lax.all_gather(arranged, 'wide', axis=2, tiled=True)  63.7 us
    all_to_all x1, blocking collectives, on_device(): lax.all_to_all(spectra[:, :, None, :], ('narrow', 'pol'), split_axis=0, c...  17 us
    another operation x1, other arithmetic  8.54 us
    ppermute x1, starting transfers between devices, passed_along(): return lax.ppermute(block, axis, route)  5.84 us
    another operation x1, local copies, waits for them, and re-layouts, fourier_table(): table = jnp.stack([jnp.cos(phase), -jnp.sin(phase)], axis=2)  4.05 us
    convert_element_type x1, local copies, waits for them, and re-layouts, fourier_table(): return table.reshape(length, 2 * channels).astype(jnp.bfloat16)  2.76 us
  transfers between devices with their start and end apart: 2, of which 2 were waited for; matrix products, arithmetic and copies ran while one was open for 12% of the time, Pallas kernels for 0%

commit v1 on v0

--- a/solution.py
+++ b/solution.py
@@ -1,13 +1,20 @@
+import functools
 import math
 
 import jax
 import jax.numpy as jnp
+import ml_dtypes
+import numpy as np
 from jax import lax
+from jax.experimental import pallas as pl
+from jax.experimental.pallas import tpu as pltpu
 from jax.sharding import PartitionSpec as P
 
 CHAN = 512
 OUTCH = 16
 BLOCK = 256
+MESH = pl.DeviceIdType.MESH
+CHUNKS = 4
 
 
 def passed_along(block, axis, distance):
@@ -88,9 +95,288 @@
     return visible
 
 
+def table_constant(length, parts):
+    channels = length // 2
+    pos = np.arange(length, dtype=np.int64)[:, None] * np.arange(channels, dtype=np.int64)[None, :]
+    phase = (pos % length).astype(np.float64) * (2.0 * math.pi / length)
+    both = np.stack([np.cos(phase), -np.sin(phase)], axis=1)
+    both = both.reshape(length, 2, parts, channels // parts).transpose(0, 2, 1, 3)
+    return both.reshape(length, 2 * channels).astype(ml_dtypes.bfloat16)
+
+
+def correlator(
+    sizes,
+    volt_ref, window_ref, table_hbm, pairs_ref, assign_ref,
+    out_ref,
+    raw, table, filt, stage, spec, total,
+    load_sem, zsend, zrecv, xsend, xrecv,
+):
+    nz, nx, npol, rows, taps, length, averaged = sizes
+    nd = nx * npol
+    part = length // nd
+    half = part // 2
+    frames = volt_ref.shape[1] // length
+    chunk = rows // CHUNKS
+    z = lax.axis_index("wide")
+    x = lax.axis_index("narrow")
+    c = lax.axis_index("pol")
+    me = x * npol + c
+
+    load_v = pltpu.make_async_copy(volt_ref, raw.at[z], load_sem.at[0])
+    load_t = pltpu.make_async_copy(table_hbm, table, load_sem.at[1])
+    load_v.start()
+    load_t.start()
+
+    def peer(j):
+        other = lax.rem(me + j, nd)
+        return other, {"narrow": lax.div(other, npol), "pol": lax.rem(other, npol)}
+
+    barrier = pltpu.get_barrier_semaphore()
+    for j in range(1, nd):
+        pl.semaphore_signal(barrier, inc=1, device_id=peer(j)[1], device_id_type=MESH)
+
+    @pl.when(z > 0)
+    def _():
+        pl.semaphore_signal(barrier, inc=1, device_id={"wide": z - 1}, device_id_type=MESH)
+
+    @pl.when(z < nz - 1)
+    def _():
+        pl.semaphore_signal(barrier, inc=1, device_id={"wide": z + 1}, device_id_type=MESH)
+
+    near = (z > 0).astype(jnp.int32) + (z < nz - 1).astype(jnp.int32)
+    pl.semaphore_wait(barrier, nd - 1 + near)
+
+    def along(direction, s, r):
+        rs = pl.ds(pl.multiple_of(r * chunk, chunk), chunk)
+        target = z + 1 if direction == 0 else z - 1
+        return pltpu.make_async_remote_copy(
+            src_ref=raw.at[s, rs, :],
+            dst_ref=raw.at[s, rs, :],
+            send_sem=zsend.at[direction, s, r],
+            recv_sem=zrecv.at[s, r],
+            device_id={"wide": target},
+            device_id_type=MESH,
+        )
+
+    def across(j, s, r, src=None):
+        rs = pl.ds(pl.multiple_of(r * chunk, chunk), chunk)
+        other, device = peer(j)
+        sender = me if src is None else src
+        return pltpu.make_async_remote_copy(
+            src_ref=stage.at[s, other, :, rs, :],
+            dst_ref=spec.at[s, sender, :, rs, :],
+            send_sem=xsend.at[s, r, j],
+            recv_sem=xrecv.at[s, r, sender],
+            device_id=device,
+            device_id_type=MESH,
+        )
+
+    load_v.wait()
+
+    def own(r, _):
+        @pl.when(z < nz - 1)
+        def _():
+            along(0, z, r).start()
+
+        @pl.when(z > 0)
+        def _():
+            along(1, z, r).start()
+
+        return 0
+
+    lax.fori_loop(0, CHUNKS, own, 0)
+    total[...] = jnp.zeros_like(total)
+    load_t.wait()
+
+    def channelize(s, r):
+        rs = pl.ds(pl.multiple_of(r * chunk, chunk), chunk)
+        earlier = jnp.maximum(s - 1, 0)
+        live = jnp.where(s > 0, 1.0, 0.0).astype(jnp.float32)
+        wide = 256
+        for k in range(0, length, wide):
+            part_of = []
+            for f in range(frames):
+                part_of.append(raw[earlier, rs, f * length + k : f * length + k + wide].astype(jnp.float32) * live)
+            for f in range(frames):
+                part_of.append(raw[s, rs, f * length + k : f * length + k + wide].astype(jnp.float32))
+            for m in range(frames):
+                first = frames + m - (taps - 1)
+                value = window_ref[0:1, k : k + wide] * part_of[first]
+                for t in range(1, taps):
+                    value = value + window_ref[t : t + 1, k : k + wide] * part_of[first + t]
+                filt[m * chunk : (m + 1) * chunk, k : k + wide] = value.astype(jnp.bfloat16)
+        for d in range(nd):
+            out = jnp.dot(
+                filt[...], table[:, d * part : (d + 1) * part], preferred_element_type=jnp.float32
+            ).astype(jnp.bfloat16)
+            stage[s, d, :, rs, :] = out.reshape(frames, chunk, part)
+        for j in range(1, nd):
+            across(j, s, r).start()
+        spec[s, me, :, rs, :] = stage[s, me, :, rs, :]
+
+    number = assign_ref[z, 0]
+    safe = jnp.maximum(number, 0)
+    row = pairs_ref[safe, 0]
+    column = pairs_ref[safe, 1]
+    per_block = BLOCK // rows
+
+    def correlate(s):
+        for j in range(1, nd):
+            src = lax.rem(me + j, nd)
+            for r in range(CHUNKS):
+                across(j, s, r, src).wait_recv()
+        lane = lax.broadcasted_iota(jnp.int32, (1, part), 1)
+        lane = jnp.where(lane >= half, lane - half, lane)
+        for m in range(frames):
+            left = right = None
+            for b in range(nd // per_block):
+                block = spec[s, b * per_block : (b + 1) * per_block, m].reshape(BLOCK, part)
+                left = block if b == 0 else jnp.where(row == b, block, left)
+                right = block if b == 0 else jnp.where(column == b, block, right)
+            turned = jnp.concatenate([-right[:, half:], right[:, :half]], axis=1)
+            for o in range(half // averaged):
+                keep = jnp.where((lane >= o * averaged) & (lane < (o + 1) * averaged), 1.0, 0.0)
+                kept = left * keep.astype(jnp.bfloat16)
+                for side, value in ((0, right), (1, turned)):
+                    total[o, :, side * BLOCK : (side + 1) * BLOCK] += lax.dot_general(
+                        kept, value, (((1,), (1,)), ((), ())), preferred_element_type=jnp.float32
+                    )
+
+    def candidate(d, i):
+        s = jnp.where(i == 0, z - d + 1, jnp.where(i == 1, 0, z + d))
+        valid = jnp.where(
+            i == 0,
+            jnp.logical_and(d > 0, z - d >= 0).astype(jnp.int32),
+            jnp.where(i == 1, (z == d).astype(jnp.int32), jnp.logical_and(d > 0, z + d < nz).astype(jnp.int32)),
+        )
+        return jnp.clip(s, 0, nz - 1), valid
+
+    def step(d, _):
+        def arrive(r, _):
+            @pl.when(jnp.logical_and(d > 0, z - d >= 0))
+            def _():
+                along(0, z - d, r).wait_recv()
+
+                @pl.when(z < nz - 1)
+                def _():
+                    along(0, z - d, r).start()
+
+            @pl.when(jnp.logical_and(d > 0, z + d < nz))
+            def _():
+                along(1, z + d, r).wait_recv()
+
+                @pl.when(z > 0)
+                def _():
+                    along(1, z + d, r).start()
+
+            def one(i, _):
+                s, valid = candidate(d, i)
+
+                @pl.when(valid == 1)
+                def _():
+                    channelize(s, r)
+
+                return 0
+
+            lax.fori_loop(0, 3, one, 0)
+            return 0
+
+        @pl.when(d < nz)
+        def _():
+            lax.fori_loop(0, CHUNKS, arrive, 0)
+
+        def add(i, _):
+            s, valid = candidate(d - 1, i)
+
+            @pl.when(jnp.logical_and(d > 0, valid == 1))
+            def _():
+                correlate(s)
+
+            return 0
+
+        lax.fori_loop(0, 3, add, 0)
+        return 0
+
+    lax.fori_loop(0, nz + 1, step, 0)
+
+    scale = jnp.where(number >= 0, 1.0, 0.0).astype(jnp.float32) * (1.0 / (nz * frames * averaged))
+    out_ref[...] = (total[...] * scale).astype(jnp.bfloat16)
+
+    def drain(r, _):
+        for s in range(nz):
+            @pl.when(jnp.logical_and(z < nz - 1, s <= z))
+            def _():
+                along(0, s, r).wait_send()
+
+            @pl.when(jnp.logical_and(z > 0, s >= z))
+            def _():
+                along(1, s, r).wait_send()
+
+            for j in range(1, nd):
+                across(j, s, r).wait_send()
+        return 0
+
+    lax.fori_loop(0, CHUNKS, drain, 0)
+
+
+def fused(voltages, pfb_window, tile_pairs, assign):
+    rows, samples = voltages.shape
+    taps, length = pfb_window.shape
+    nz, nx, npol = (lax.axis_size(a) for a in ("wide", "narrow", "pol"))
+    nd = nx * npol
+    frames = samples // length
+    averaged = CHAN // OUTCH
+    part = length // nd
+    outs = part // 2 // averaged
+    chunk = rows // CHUNKS
+    sizes = (nz, nx, npol, rows, taps, length, averaged)
+    visible = pl.pallas_call(
+        functools.partial(correlator, sizes),
+        out_shape=jax.ShapeDtypeStruct((outs, BLOCK, 2 * BLOCK), jnp.bfloat16),
+        in_specs=[
+            pl.BlockSpec(memory_space=pl.ANY),
+            pl.BlockSpec(memory_space=pltpu.VMEM),
+            pl.BlockSpec(memory_space=pl.ANY),
+            pl.BlockSpec(memory_space=pltpu.SMEM),
+            pl.BlockSpec(memory_space=pltpu.SMEM),
+        ],
+        out_specs=pl.BlockSpec(memory_space=pltpu.VMEM),
+        scratch_shapes=[
+            pltpu.VMEM((nz, rows, samples), jnp.bfloat16),
+            pltpu.VMEM((length, length), jnp.bfloat16),
+            pltpu.VMEM((frames * chunk, length), jnp.bfloat16),
+            pltpu.VMEM((nz, nd, frames, rows, part), jnp.bfloat16),
+            pltpu.VMEM((nz, nd, frames, rows, part), jnp.bfloat16),
+            pltpu.VMEM((outs, BLOCK, 2 * BLOCK), jnp.float32),
+            pltpu.SemaphoreType.DMA((2,)),
+            pltpu.SemaphoreType.DMA((2, nz, CHUNKS)),
+            pltpu.SemaphoreType.DMA((nz, CHUNKS)),
+            pltpu.SemaphoreType.DMA((nz, CHUNKS, nd)),
+            pltpu.SemaphoreType.DMA((nz, CHUNKS, nd)),
+        ],
+        compiler_params=pltpu.CompilerParams(
+            collective_id=0, has_side_effects=True, vmem_limit_bytes=40 * 1024 * 1024
+        ),
+        cost_estimate=pl.CostEstimate(flops=10**10, bytes_accessed=10**7, transcendentals=0),
+    )(voltages, pfb_window, jnp.asarray(table_constant(length, nd)), tile_pairs, assign)
+    return visible.reshape(1, outs, BLOCK, 2, BLOCK)
+
+
 def solution(mesh):
     in_specs = (P(("groups", "narrow", "pol"), "wide"), P(), P(), P())
     out_specs = P(("groups", "wide"), ("narrow", "pol"), None, None, None)
-    return jax.shard_map(
-        on_device, mesh=mesh, in_specs=in_specs, out_specs=out_specs, check_vma=False
-    )
+
+    def run(voltages, pfb_window, tile_pairs, assign):
+        rows, samples = voltages.shape
+        taps, length = pfb_window.shape
+        part = length // (lax.axis_size("narrow") * lax.axis_size("pol"))
+        fits = (
+            part % 256 == 0
+            and assign.shape[1] == 1
+            and BLOCK % rows == 0
+            and rows % (16 * CHUNKS) == 0
+            and samples // length >= taps - 1
+        )
+        return (fused if fits else on_device)(voltages, pfb_window, tile_pairs, assign)
+
+    return jax.shard_map(run, mesh=mesh, in_specs=in_specs, out_specs=out_specs, check_vma=False)

time: 132 us -> 69.8 us (0.53)
  waiting for transfers between devices: 64 us -> 0 us
  Pallas kernels: 0 us -> 63.3 us
  blocking collectives: 17 us -> 0 us
  between operations: 14.1 us -> 0.01 us
  other arithmetic: 12.3 us -> 0 us
  local copies, waits for them, and re-layouts: 13.7 us -> 6.05 us
  starting transfers between devices: 5.84 us -> 0 us
  matrix products: 2.48 us -> 0 us
  loops' own time: 2.16 us -> 0 us
    all_gather x1 -> x0, waiting for transfers between devices: 63.7 us -> none  [on_device(): whole = lax.all_gather(arranged, 'wide', axis=2, tiled=True)]
    pallas_call x0 -> x1, Pallas kernels: none -> 63.3 us  [fused(): pl.pallas_call(functools.partial(correlator, sizes), out_shape=jax.ShapeD...]
    all_to_all x1 -> x0, blocking collectives: 17 us -> none  [on_device(): lax.all_to_all(spectra[:, :, None, :], ('narrow', 'pol'), split_axis=0, c...]
    another operation x2 -> x0, other arithmetic: 8.73 us -> none
    ppermute x1 -> x0, starting transfers between devices: 5.84 us -> none  [passed_along(): return lax.ppermute(block, axis, route)]
    another operation x1 -> x0, local copies, waits for them, and re-layouts: 4.05 us -> none  [fourier_table(): table = jnp.stack([jnp.cos(phase), -jnp.sin(phase)], axis=2)]
    convert_element_type x2 -> x0, local copies, waits for them, and re-layouts: 3.87 us -> none  [the longest x1 2.76 us: fourier_table(): return table.reshape(length, 2 * channels).astype(jnp.bfloat16)]
    unnamed x7 -> x8, local copies, waits for them, and re-layouts: 1.53 us -> 4.94 us
  transfers between devices with their start and end apart: 2 -> 0, of which waited for: 2 -> 0; matrix products, arithmetic and copies ran while one was open for 12% -> 0% of each run, Pallas kernels for 0% -> 0%
where the time goes in v1:
time: 69.8 us; the launch traced here: 69.4 us
  Pallas kernels  63.3 us (91%)
  local copies, waits for them, and re-layouts  6.05 us (9%)
    pallas_call x1, Pallas kernels, fused(): pl.pallas_call(functools.partial(correlator, sizes), out_shape=jax.ShapeD...  63.3 us
    unnamed x8, local copies, waits for them, and re-layouts  4.94 us

profile of v1, /device:TPU:0, one launch (start us, length us, event | category | flops | bytes accessed | tf_op | source)
XLA Modules:
  0.0 69.4 jit_solution(12491330290923791878)
XLA Ops:
  0.0 0.8 %copy.6.pairs_ref = s32[3,2]{1,0:T(4,128)S(1)} copy(s32[3,2]{0,1:T(2,128)} %param.7) | data formatting | bytes 48 | tf_op args[2]
  0.8 0.7 %copy.7.assign_ref = s32[4,1]{1,0:T(4,128)S(1)} copy(s32[4,1]{0,1:T(1,128)} %param.8) | data formatting | bytes 32 | tf_op args[3]
  1.5 0.0 copy-start
  1.5 1.1 %copy-done = bf16[128,3072]{1,0:T(8,128)(2,1)S(1)} copy-done((bf16[128,3072]{1,0:T(8,128)(2,1)S(1)}, bf16[128,3072]{1,0:T(8,128)(2,1)}, u32[]{:S(2)}) %copy-start) | copy-done | bytes 786456
  2.6 0.0 copy-start.1
  2.6 0.7 %copy-done.1 = f32[4,1024]{1,0:T(4,128)S(1)} copy-done((f32[4,1024]{1,0:T(4,128)S(1)}, f32[4,1024]{1,0:T(4,128)}, u32[]{:S(2)}) %copy-start.1) | copy-done | bytes 16408
  3.4 0.0 copy-start.2
  3.4 1.6 %copy-done.2 = bf16[1024,1024]{1,0:T(8,128)(2,1)S(1)} copy-done((bf16[1024,1024]{1,0:T(8,128)(2,1)S(1)}, bf16[1024,1024]{1,0:T(8,128)(2,1)}, u32[]{:S(2)}) %copy-start.2) | copy-done | bytes 2097176
  4.9 63.3 %shard_map.55 = bf16[4,256,512]{2,1,0:T(8,128)(2,1)S(1)} custom-call(bf16[128,3072]{1,0:T(8,128)(2,1)S(1)} %copy-done, f32[4,1024]{1,0:T(4,128)S(1)} %copy-done.1, bf16[1024,1024]{1,0:T(8,128)(2,1)S(1)} %copy-done.2, s32[3,2]{1,0:T(4,128)S(1)} %copy.6.pairs_ref, s32[4,1]{1,0:T(4,128)S(1)} %copy.7.assign_ref), custom_call_target="tpu_custom_call" | custom-call | flops 10000000000 | bytes 10000000 | tf_op jit(solution)/shard_map/pallas_call | solution.py:333
  68.3 1.1 %reshape.3 = bf16[1,4,256,2,256]{4,3,2,1,0:T(2,128)(2,1)} reshape(bf16[4,256,512]{2,1,0:T(8,128)(2,1)S(1)} %shard_map.55) | data formatting | bytes 2097152 | tf_op jit(solution)/shard_map/reshape | solution.py:362
Async XLA Ops:
  1.5 1.1 %copy-start = (bf16[128,3072]{1,0:T(8,128)(2,1)S(1)}, bf16[128,3072]{1,0:T(8,128)(2,1)}, u32[]{:S(2)}) copy-start(bf16[128,3072]{1,0:T(8,128)(2,1)} %volt_ref.1) | copy-start | bytes 2359300
  2.6 0.7 %copy-start.1 = (f32[4,1024]{1,0:T(4,128)S(1)}, f32[4,1024]{1,0:T(4,128)}, u32[]{:S(2)}) copy-start(f32[4,1024]{1,0:T(4,128)} %window_ref.1) | copy-start | bytes 49156
  3.4 1.6 %copy-start.2 = (bf16[1024,1024]{1,0:T(8,128)(2,1)S(1)}, bf16[1024,1024]{1,0:T(8,128)(2,1)}, u32[]{:S(2)}) copy-start(bf16[1024,1024]{1,0:T(8,128)(2,1)} %constant.2.clone.table_hbm) | copy-start | bytes 6291460

commit v2 on v1

--- a/solution.py
+++ b/solution.py
@@ -106,9 +106,9 @@
 
 def correlator(
     sizes,
-    volt_ref, window_ref, table_hbm, pairs_ref, assign_ref,
+    volt_ref, window_hbm, table_hbm, pairs_ref, assign_ref,
     out_ref,
-    raw, table, filt, stage, spec, total,
+    raw, window_ref, table, filt, stage, spec, total,
     load_sem, zsend, zrecv, xsend, xrecv,
 ):
     nz, nx, npol, rows, taps, length, averaged = sizes
@@ -124,7 +124,9 @@
 
     load_v = pltpu.make_async_copy(volt_ref, raw.at[z], load_sem.at[0])
     load_t = pltpu.make_async_copy(table_hbm, table, load_sem.at[1])
+    load_w = pltpu.make_async_copy(window_hbm, window_ref, load_sem.at[2])
     load_v.start()
+    load_w.start()
     load_t.start()
 
     def peer(j):
@@ -186,6 +188,7 @@
 
     lax.fori_loop(0, CHUNKS, own, 0)
     total[...] = jnp.zeros_like(total)
+    load_w.wait()
     load_t.wait()
 
     def channelize(s, r):
@@ -214,10 +217,10 @@
             across(j, s, r).start()
         spec[s, me, :, rs, :] = stage[s, me, :, rs, :]
 
-    number = assign_ref[z, 0]
+    number = assign_ref[0, z]
     safe = jnp.maximum(number, 0)
-    row = pairs_ref[safe, 0]
-    column = pairs_ref[safe, 1]
+    row = pairs_ref[0, safe]
+    column = pairs_ref[1, safe]
     per_block = BLOCK // rows
 
     def correlate(s):
@@ -225,22 +228,29 @@
             src = lax.rem(me + j, nd)
             for r in range(CHUNKS):
                 across(j, s, r, src).wait_recv()
-        lane = lax.broadcasted_iota(jnp.int32, (1, part), 1)
-        lane = jnp.where(lane >= half, lane - half, lane)
+        lefts, rights, turned = [], [], []
         for m in range(frames):
             left = right = None
             for b in range(nd // per_block):
                 block = spec[s, b * per_block : (b + 1) * per_block, m].reshape(BLOCK, part)
                 left = block if b == 0 else jnp.where(row == b, block, left)
                 right = block if b == 0 else jnp.where(column == b, block, right)
-            turned = jnp.concatenate([-right[:, half:], right[:, :half]], axis=1)
-            for o in range(half // averaged):
-                keep = jnp.where((lane >= o * averaged) & (lane < (o + 1) * averaged), 1.0, 0.0)
-                kept = left * keep.astype(jnp.bfloat16)
-                for side, value in ((0, right), (1, turned)):
-                    total[o, :, side * BLOCK : (side + 1) * BLOCK] += lax.dot_general(
-                        kept, value, (((1,), (1,)), ((), ())), preferred_element_type=jnp.float32
-                    )
+            lefts.append(left)
+            rights.append(right)
+            turned += [-right[:, half:], right[:, :half]]
+        left = jnp.concatenate(lefts, axis=1)
+        both = jnp.concatenate(
+            [jnp.concatenate(rights, axis=1), jnp.concatenate(turned, axis=1)], axis=0
+        )
+        lane = lax.rem(lax.broadcasted_iota(jnp.int32, (1, frames * part), 1), half)
+        for o in range(half // averaged):
+            keep = jnp.where((lane >= o * averaged) & (lane < (o + 1) * averaged), 1.0, 0.0)
+            total[o] += lax.dot_general(
+                left * keep.astype(jnp.bfloat16),
+                both,
+                (((1,), (1,)), ((), ())),
+                preferred_element_type=jnp.float32,
+            )
 
     def candidate(d, i):
         s = jnp.where(i == 0, z - d + 1, jnp.where(i == 1, 0, z + d))
@@ -279,22 +289,23 @@
                 return 0
 
             lax.fori_loop(0, 3, one, 0)
+
+            def add(i, _):
+                s, valid = candidate(d - 1, i)
+
+                @pl.when(jnp.logical_and(d > 0, valid == 1))
+                def _():
+                    correlate(s)
+
+                return 0
+
+            @pl.when(r == 1)
+            def _():
+                lax.fori_loop(0, 3, add, 0)
+
             return 0
 
-        @pl.when(d < nz)
-        def _():
-            lax.fori_loop(0, CHUNKS, arrive, 0)
-
-        def add(i, _):
-            s, valid = candidate(d - 1, i)
-
-            @pl.when(jnp.logical_and(d > 0, valid == 1))
-            def _():
-                correlate(s)
-
-            return 0
-
-        lax.fori_loop(0, 3, add, 0)
+        lax.fori_loop(0, CHUNKS, arrive, 0)
         return 0
 
     lax.fori_loop(0, nz + 1, step, 0)
@@ -334,21 +345,22 @@
         functools.partial(correlator, sizes),
         out_shape=jax.ShapeDtypeStruct((outs, BLOCK, 2 * BLOCK), jnp.bfloat16),
         in_specs=[
-            pl.BlockSpec(memory_space=pl.ANY),
-            pl.BlockSpec(memory_space=pltpu.VMEM),
-            pl.BlockSpec(memory_space=pl.ANY),
+            pl.BlockSpec(memory_space=pltpu.HBM),
+            pl.BlockSpec(memory_space=pltpu.HBM),
+            pl.BlockSpec(memory_space=pltpu.HBM),
             pl.BlockSpec(memory_space=pltpu.SMEM),
             pl.BlockSpec(memory_space=pltpu.SMEM),
         ],
         out_specs=pl.BlockSpec(memory_space=pltpu.VMEM),
         scratch_shapes=[
             pltpu.VMEM((nz, rows, samples), jnp.bfloat16),
+            pltpu.VMEM((taps, length), jnp.float32),
             pltpu.VMEM((length, length), jnp.bfloat16),
             pltpu.VMEM((frames * chunk, length), jnp.bfloat16),
             pltpu.VMEM((nz, nd, frames, rows, part), jnp.bfloat16),
             pltpu.VMEM((nz, nd, frames, rows, part), jnp.bfloat16),
             pltpu.VMEM((outs, BLOCK, 2 * BLOCK), jnp.float32),
-            pltpu.SemaphoreType.DMA((2,)),
+            pltpu.SemaphoreType.DMA((3,)),
             pltpu.SemaphoreType.DMA((2, nz, CHUNKS)),
             pltpu.SemaphoreType.DMA((nz, CHUNKS)),
             pltpu.SemaphoreType.DMA((nz, CHUNKS, nd)),
@@ -358,7 +370,7 @@
             collective_id=0, has_side_effects=True, vmem_limit_bytes=40 * 1024 * 1024
         ),
         cost_estimate=pl.CostEstimate(flops=10**10, bytes_accessed=10**7, transcendentals=0),
-    )(voltages, pfb_window, jnp.asarray(table_constant(length, nd)), tile_pairs, assign)
+    )(voltages, pfb_window, jnp.asarray(table_constant(length, nd)), tile_pairs.T, assign.T)
     return visible.reshape(1, outs, BLOCK, 2, BLOCK)
 
 

time: 69.8 us -> 69.8 us (level)
    unnamed x8 -> x10, local copies, waits for them, and re-layouts: 4.94 us -> 4.77 us
where the time goes in v2:
time: 69.8 us; the launch traced here: 69.4 us
  Pallas kernels  63.5 us (91%)
  local copies, waits for them, and re-layouts  5.88 us (8%)
    pallas_call x1, Pallas kernels, fused(): pl.pallas_call(functools.partial(correlator, sizes), out_shape=jax.ShapeD...  63.5 us
    unnamed x10, local copies, waits for them, and re-layouts  4.77 us

profile of v2, /device:TPU:0, one launch (start us, length us, event | category | flops | bytes accessed | tf_op | source)
XLA Modules:
  0.0 69.4 jit_solution(2439421545110309242)
XLA Ops:
  0.0 0.0 copy-start
  0.0 1.1 %copy-done = bf16[128,3072]{1,0:T(8,128)(2,1)S(1)} copy-done((bf16[128,3072]{1,0:T(8,128)(2,1)S(1)}, bf16[128,3072]{1,0:T(8,128)(2,1)}, u32[]{:S(2)}) %copy-start) | copy-done | bytes 786456
  1.1 0.0 copy-start.1
  1.1 0.7 %copy-done.1 = f32[4,1024]{1,0:T(4,128)S(1)} copy-done((f32[4,1024]{1,0:T(4,128)S(1)}, f32[4,1024]{1,0:T(4,128)}, u32[]{:S(2)}) %copy-start.1) | copy-done | bytes 16408
  1.9 0.0 copy-start.2
  1.9 0.7 copy-done.2
  2.5 0.0 copy-start.3
  2.5 0.7 copy-done.3
  3.2 0.0 copy-start.4
  3.2 1.6 %copy-done.4 = bf16[1024,1024]{1,0:T(8,128)(2,1)S(1)} copy-done((bf16[1024,1024]{1,0:T(8,128)(2,1)S(1)}, bf16[1024,1024]{1,0:T(8,128)(2,1)}, u32[]{:S(2)}) %copy-start.4) | copy-done | bytes 2097176
  4.8 63.5 %shard_map.55 = bf16[4,256,512]{2,1,0:T(8,128)(2,1)S(1)} custom-call(bf16[128,3072]{1,0:T(8,128)(2,1)S(1)} %copy-done, f32[4,1024]{1,0:T(4,128)S(1)} %copy-done.1, bf16[1024,1024]{1,0:T(8,128)(2,1)S(1)} %copy-done.4, s32[2,3]{1,0:T(2,128)S(1)} %bitcast.2, s32[1,4]{1,0:T(1,128)S(1)} %bitcast.3), custom_call_target="tpu_custom_call" | custom-call | flops 10000000000 | bytes 10000000 | tf_op jit(solution)/shard_map/pallas_call | solution.py:344
  68.3 1.1 %reshape.3 = bf16[1,4,256,2,256]{4,3,2,1,0:T(2,128)(2,1)} reshape(bf16[4,256,512]{2,1,0:T(8,128)(2,1)S(1)} %shard_map.55) | data formatting | bytes 2097152 | tf_op jit(solution)/shard_map/reshape | solution.py:374
Async XLA Ops:
  0.0 1.1 %copy-start = (bf16[128,3072]{1,0:T(8,128)(2,1)S(1)}, bf16[128,3072]{1,0:T(8,128)(2,1)}, u32[]{:S(2)}) copy-start(bf16[128,3072]{1,0:T(8,128)(2,1)} %volt_ref.1) | copy-start | bytes 2359300
  1.1 0.7 %copy-start.1 = (f32[4,1024]{1,0:T(4,128)S(1)}, f32[4,1024]{1,0:T(4,128)}, u32[]{:S(2)}) copy-start(f32[4,1024]{1,0:T(4,128)} %window_hbm.1) | copy-start | bytes 49156
  1.9 0.7 copy-start.2
  2.5 0.7 copy-start.3
  3.2 1.6 %copy-start.4 = (bf16[1024,1024]{1,0:T(8,128)(2,1)S(1)}, bf16[1024,1024]{1,0:T(8,128)(2,1)}, u32[]{:S(2)}) copy-start(bf16[1024,1024]{1,0:T(8,128)(2,1)} %constant.2.clone.table_hbm) | copy-start | bytes 6291460

commit v3 on v2

--- a/solution.py
+++ b/solution.py
@@ -14,7 +14,8 @@
 OUTCH = 16
 BLOCK = 256
 MESH = pl.DeviceIdType.MESH
-CHUNKS = 4
+SHARES = (1, 1, 1, 1)
+CHUNKS = len(SHARES)
 
 
 def passed_along(block, axis, distance):
@@ -116,7 +117,8 @@
     part = length // nd
     half = part // 2
     frames = volt_ref.shape[1] // length
-    chunk = rows // CHUNKS
+    unit = rows // sum(SHARES)
+    pieces = [pl.ds(unit * sum(SHARES[:r]), unit * SHARES[r]) for r in range(CHUNKS)]
     z = lax.axis_index("wide")
     x = lax.axis_index("narrow")
     c = lax.axis_index("pol")
@@ -148,11 +150,11 @@
     near = (z > 0).astype(jnp.int32) + (z < nz - 1).astype(jnp.int32)
     pl.semaphore_wait(barrier, nd - 1 + near)
 
-    def along(direction, s, r):
-        rs = pl.ds(pl.multiple_of(r * chunk, chunk), chunk)
+    def along(direction, s, r, first=False):
+        rs = pieces[r]
         target = z + 1 if direction == 0 else z - 1
         return pltpu.make_async_remote_copy(
-            src_ref=raw.at[s, rs, :],
+            src_ref=(volt_ref.at[rs, :] if first else raw.at[s, rs, :]),
             dst_ref=raw.at[s, rs, :],
             send_sem=zsend.at[direction, s, r],
             recv_sem=zrecv.at[s, r],
@@ -161,7 +163,7 @@
         )
 
     def across(j, s, r, src=None):
-        rs = pl.ds(pl.multiple_of(r * chunk, chunk), chunk)
+        rs = pieces[r]
         other, device = peer(j)
         sender = me if src is None else src
         return pltpu.make_async_remote_copy(
@@ -173,26 +175,25 @@
             device_id_type=MESH,
         )
 
-    load_v.wait()
-
-    def own(r, _):
+    def own(r):
         @pl.when(z < nz - 1)
         def _():
-            along(0, z, r).start()
+            along(0, z, r, True).start()
 
         @pl.when(z > 0)
         def _():
-            along(1, z, r).start()
-
-        return 0
-
-    lax.fori_loop(0, CHUNKS, own, 0)
+            along(1, z, r, True).start()
+
+    for r in range(CHUNKS):
+        own(r)
     total[...] = jnp.zeros_like(total)
+    load_v.wait()
     load_w.wait()
     load_t.wait()
 
     def channelize(s, r):
-        rs = pl.ds(pl.multiple_of(r * chunk, chunk), chunk)
+        rs = pieces[r]
+        chunk = unit * SHARES[r]
         earlier = jnp.maximum(s - 1, 0)
         live = jnp.where(s > 0, 1.0, 0.0).astype(jnp.float32)
         wide = 256
@@ -210,7 +211,7 @@
                 filt[m * chunk : (m + 1) * chunk, k : k + wide] = value.astype(jnp.bfloat16)
         for d in range(nd):
             out = jnp.dot(
-                filt[...], table[:, d * part : (d + 1) * part], preferred_element_type=jnp.float32
+                filt[0 : frames * chunk], table[:, d * part : (d + 1) * part], preferred_element_type=jnp.float32
             ).astype(jnp.bfloat16)
             stage[s, d, :, rs, :] = out.reshape(frames, chunk, part)
         for j in range(1, nd):
@@ -262,7 +263,7 @@
         return jnp.clip(s, 0, nz - 1), valid
 
     def step(d, _):
-        def arrive(r, _):
+        def arrive(r):
             @pl.when(jnp.logical_and(d > 0, z - d >= 0))
             def _():
                 along(0, z - d, r).wait_recv()
@@ -299,13 +300,11 @@
 
                 return 0
 
-            @pl.when(r == 1)
-            def _():
+            if r == 1:
                 lax.fori_loop(0, 3, add, 0)
 
-            return 0
-
-        lax.fori_loop(0, CHUNKS, arrive, 0)
+        for r in range(CHUNKS):
+            arrive(r)
         return 0
 
     lax.fori_loop(0, nz + 1, step, 0)
@@ -313,7 +312,7 @@
     scale = jnp.where(number >= 0, 1.0, 0.0).astype(jnp.float32) * (1.0 / (nz * frames * averaged))
     out_ref[...] = (total[...] * scale).astype(jnp.bfloat16)
 
-    def drain(r, _):
+    def drain(r):
         for s in range(nz):
             @pl.when(jnp.logical_and(z < nz - 1, s <= z))
             def _():
@@ -325,9 +324,9 @@
 
             for j in range(1, nd):
                 across(j, s, r).wait_send()
-        return 0
-
-    lax.fori_loop(0, CHUNKS, drain, 0)
+
+    for r in range(CHUNKS):
+        drain(r)
 
 
 def fused(voltages, pfb_window, tile_pairs, assign):
@@ -339,7 +338,7 @@
     averaged = CHAN // OUTCH
     part = length // nd
     outs = part // 2 // averaged
-    chunk = rows // CHUNKS
+    chunk = rows // sum(SHARES) * max(SHARES)
     sizes = (nz, nx, npol, rows, taps, length, averaged)
     visible = pl.pallas_call(
         functools.partial(correlator, sizes),
@@ -367,7 +366,7 @@
             pltpu.SemaphoreType.DMA((nz, CHUNKS, nd)),
         ],
         compiler_params=pltpu.CompilerParams(
-            collective_id=0, has_side_effects=True, vmem_limit_bytes=40 * 1024 * 1024
+            collective_id=0, has_side_effects=True, vmem_limit_bytes=60 * 1024 * 1024
         ),
         cost_estimate=pl.CostEstimate(flops=10**10, bytes_accessed=10**7, transcendentals=0),
     )(voltages, pfb_window, jnp.asarray(table_constant(length, nd)), tile_pairs.T, assign.T)
@@ -386,7 +385,7 @@
             part % 256 == 0
             and assign.shape[1] == 1
             and BLOCK % rows == 0
-            and rows % (16 * CHUNKS) == 0
+            and rows % (16 * sum(SHARES)) == 0
             and samples // length >= taps - 1
         )
         return (fused if fits else on_device)(voltages, pfb_window, tile_pairs, assign)

time: 69.8 us -> 67 us (0.960)
  local copies, waits for them, and re-layouts: 5.88 us -> 2.14 us
  Pallas kernels: 63.5 us -> 64.6 us
    unnamed x10 -> x0, local copies, waits for them, and re-layouts: 4.77 us -> none
    pallas_call x1, Pallas kernels: 63.5 us -> 64.6 us  [fused(): pl.pallas_call(functools.partial(correlator, sizes), out_shape=jax.ShapeD...]
    reshape x1, local copies, waits for them, and re-layouts: 1.11 us -> 2.14 us  [fused(): return visible.reshape(1, outs, BLOCK, 2, BLOCK)]
where the time goes in v3:
time: 67 us; the launch traced here: 66.7 us
  Pallas kernels  64.6 us (96%)
  local copies, waits for them, and re-layouts  2.14 us (3%)
    pallas_call x1, Pallas kernels, fused(): pl.pallas_call(functools.partial(correlator, sizes), out_shape=jax.ShapeD...  64.6 us
    reshape x1, local copies, waits for them, and re-layouts, fused(): return visible.reshape(1, outs, BLOCK, 2, BLOCK)  2.14 us

profile of v3, /device:TPU:0, one launch (start us, length us, event | category | flops | bytes accessed | tf_op | source)
XLA Modules:
  0.0 66.7 jit_solution(15861766974633494367)
XLA Ops:
  0.0 64.6 %shard_map.55 = bf16[4,256,512]{2,1,0:T(8,128)(2,1)} custom-call(bf16[128,3072]{1,0:T(8,128)(2,1)} %volt_ref.1, f32[4,1024]{1,0:T(4,128)} %window_hbm.1, bf16[1024,1024]{1,0:T(8,128)(2,1)} %constant.2.clone.table_hbm, s32[2,3]{1,0:T(2,128)} %bitcast.2, s32[1,4]{1,0:T(1,128)} %bitcast.3), custom_call_target="tpu_custom_call" | custom-call | flops 10000000000 | bytes 10000000 | tf_op jit(solution)/shard_map/pallas_call | solution.py:343
  64.6 2.1 %reshape.3 = bf16[1,4,256,2,256]{4,3,2,1,0:T(2,128)(2,1)} reshape(bf16[4,256,512]{2,1,0:T(8,128)(2,1)} %shard_map.55) | data formatting | bytes 2097152 | tf_op jit(solution)/shard_map/reshape | solution.py:373
